TPU v7x, 32 devices: a whole 2x2x4 slice. The times are simulated.
32 devices in a mesh: grp: 2 (over y), edge: 4 (over z), feat: 2 (over x), rep: 2 (over core).
Axes of the slice: x: 2, y: 2, z: 4, core: 2. Of those that a mesh axis runs over, the one named last changes fastest.
Arguments:
- edge_embed: bfloat16 [8192, 512], P(('grp', 'edge'), 'feat'), parts along dimension 0, may hold values from -6 to 6
- w_down: bfloat16 [512, 64], P('feat'), may hold values from -0.25 to 0.25
- w_bilinear: bfloat16 [64, 64], replicated, may hold values from -0.75 to 0.75
- w_up: bfloat16 [64, 512], P(None, 'feat'), may hold values from -0.75 to 0.75
- w_residual: bfloat16 [2, 512, 512], replicated, may hold values from -0.25 to 0.25
- tile_coef: bfloat16 [64, 16, 128, 128], P(('grp', 'edge'), 'rep'), parts along dimension 0, may hold values from -0.125 to 0.125
- tile_source: int32 [64, 16], P('grp'), parts along dimension 0, may hold values from 0 to 31, as said below
- target_rows: int32 [8192], P(('grp', 'edge')), parts along dimension 0, may hold values from 0 to 4095, as said below
- cotangent: bfloat16 [8192, 512], P(('grp', 'edge'), 'feat'), parts along dimension 0, may hold values from -6 to 6
Outputs:
- edge_out: bfloat16 [8192, 512], P(('grp', 'edge'), 'feat'), parts along dimension 0
- grad_target: bfloat16 [8192, 512], P(('grp', 'edge'), 'feat'), parts along dimension 0
There are 2 independent parts, one for each index of `grp`. A program takes and returns all parts, laid end to end along the dimension named above; an argument that names none is the same for every part. Nothing has to cross between parts.
Inputs may be any that keep to these rules, and one draw needn't show every extreme that they name: `tile_source`: blocks t*8 to t*8 + 7 belong to index t of the edge axis; tiles r*8 to r*8 + 7 belong to index r of rep. Among the 64 tiles of one edge index and one rep index, at most 32 name blocks of any one edge index, and exactly 32 name blocks of some edge index. `target_rows`: row t = q*1024 + p*256 + l with l < 256 names a source row p*1024 + q*256 + l2 with l2 < 256; every source row is named once.
All inputs are finite; a program needn't handle non-finite values.
Results may differ from a plain program's by a relative error of at most 0.0085.
Values may be sent and summed in bfloat16 or wider, within the bound.
A program may use at most 64 MiB of HBM per device.

v0:
```python
import jax
import jax.numpy as jnp
from jax import lax
from jax.sharding import PartitionSpec as P


def silu_slope(value):
    sig = jax.nn.sigmoid(value)
    return sig * (1.0 + value * (1.0 - sig))


def feat_total(value):
    return lax.psum(value, "feat")


def rep_total(value):
    return lax.psum(value, "rep")


def trade(payload):
    return lax.all_to_all(payload, "edge", split_axis=0, concat_axis=0, tiled=True)


def contract(values, piece_weight):
    piece = lax.all_gather(values, "feat", axis=1, tiled=True)
    return jnp.dot(
        piece, piece_weight(jnp.int32(0), piece.shape[1]), preferred_element_type=jnp.float32
    )


def on_device(
    edge_embed, w_down, w_bilinear, w_up, w_residual, tile_coef, tile_source, target_rows, cotangent
):
    edges_dev, columns = edge_embed.shape
    blocks_dev, tiles_half, block_rows, _ = tile_coef.shape
    width_tri = w_down.shape[1]
    peers = lax.axis_size("edge")
    copies = lax.axis_size("rep")
    my_edge = lax.axis_index("edge")
    my_rep = lax.axis_index("rep")
    my_feat = lax.axis_index("feat")
    capacity = 2 * blocks_dev * tiles_half // peers
    entries = blocks_dev * tiles_half
    grid = tile_source.reshape(peers, blocks_dev, copies, tiles_half)
    lists = lax.dynamic_index_in_dim(grid, my_rep, axis=2, keepdims=False).reshape(peers, entries)
    owners = lists // blocks_dev
    local_ids = lists % blocks_dev
    hits = owners == my_edge
    slot_send = jnp.cumsum(hits.astype(jnp.int32), axis=1) - 1
    slot_range = jnp.arange(capacity, dtype=jnp.int32)
    picked = hits[:, :, None] & (slot_send[:, :, None] == slot_range[None, None, :])
    send_local = jnp.sum(jnp.where(picked, local_ids[:, :, None], 0), axis=1)
    send_valid = jnp.any(picked, axis=1)
    my_list = lax.dynamic_index_in_dim(lists, my_edge, 0, keepdims=False)
    my_owner = my_list // blocks_dev
    order = jnp.arange(entries, dtype=jnp.int32)
    same_before = (my_owner[:, None] == my_owner[None, :]) & (order[None, :] < order[:, None])
    my_slot = jnp.sum(same_before.astype(jnp.int32), axis=1)
    pre_down = feat_total(jnp.dot(edge_embed, w_down, preferred_element_type=jnp.float32))
    down_own = jax.nn.silu(pre_down).astype(jnp.bfloat16)
    down_blocks = down_own.reshape(blocks_dev, block_rows, width_tri)
    arrived = trade(down_blocks[send_local])
    sources = arrived[my_owner, my_slot]
    sources = sources.reshape(blocks_dev, tiles_half, block_rows, width_tri)
    partial_tri = jnp.einsum(
        "bkij,bkjc->bic", tile_coef, sources, preferred_element_type=jnp.float32
    )
    partial_tri = partial_tri.reshape(edges_dev, width_tri)
    tri_sum = rep_total(partial_tri).astype(jnp.bfloat16)
    pre_bil = jnp.dot(tri_sum, w_bilinear, preferred_element_type=jnp.float32)
    mid_act = jax.nn.silu(pre_bil).astype(jnp.bfloat16)
    hidden = (
        edge_embed.astype(jnp.float32) + jnp.dot(mid_act, w_up, preferred_element_type=jnp.float32)
    ).astype(jnp.bfloat16)
    saved = []
    for layer in range(w_residual.shape[0]):
        weight = w_residual[layer]

        def rows_piece(start, count, weight=weight):
            return lax.dynamic_slice(weight, (start, my_feat * columns), (count, columns))

        pre_res = contract(hidden, rows_piece)
        hidden = (hidden.astype(jnp.float32) + jax.nn.silu(pre_res)).astype(jnp.bfloat16)
        saved.append(pre_res)
    grad_hidden = cotangent.astype(jnp.float32)
    for layer in range(w_residual.shape[0] - 1, -1, -1):
        dz_layer = (grad_hidden * silu_slope(saved[layer])).astype(jnp.bfloat16)
        weight = w_residual[layer]

        def cols_piece(start, count, weight=weight):
            return lax.dynamic_slice(weight, (my_feat * columns, start), (columns, count)).T

        grad_hidden = grad_hidden + contract(dz_layer, cols_piece)
    grad_hb = grad_hidden.astype(jnp.bfloat16)
    grad_mid = feat_total(jnp.dot(grad_hb, w_up.T, preferred_element_type=jnp.float32))
    grad_bil = (grad_mid * silu_slope(pre_bil)).astype(jnp.bfloat16)
    grad_tri_own = jnp.dot(grad_bil, w_bilinear.T, preferred_element_type=jnp.float32).astype(
        jnp.bfloat16
    )
    grad_blocks = grad_tri_own.reshape(blocks_dev, block_rows, width_tri)
    contrib = jnp.einsum(
        "bkij,bic->bkjc", tile_coef, grad_blocks, preferred_element_type=jnp.float32
    ).astype(jnp.bfloat16)
    contrib = contrib.reshape(entries, block_rows, width_tri)
    outgoing = (
        jnp.zeros((peers, capacity, block_rows, width_tri), jnp.bfloat16)
        .at[my_owner, my_slot]
        .set(contrib)
    )
    incoming = trade(outgoing).reshape(peers * capacity, block_rows, width_tri)
    block_range = jnp.arange(blocks_dev, dtype=jnp.int32)
    select = (
        (send_local[:, :, None] == block_range[None, None, :]) & send_valid[:, :, None]
    ).astype(jnp.bfloat16)
    select = select.reshape(peers * capacity, blocks_dev)
    grad_down = jnp.einsum("sl,sjc->ljc", select, incoming, preferred_element_type=jnp.float32)
    grad_down = grad_down.reshape(edges_dev, width_tri)
    grad_down = rep_total(grad_down)
    grad_pre = (grad_down * silu_slope(pre_down)).astype(jnp.bfloat16)
    grad_edge = (
        grad_hb.astype(jnp.float32)
        + jnp.dot(grad_pre, w_down.T, preferred_element_type=jnp.float32)
    ).astype(jnp.bfloat16)
    span_rows = edges_dev // peers
    turned = lax.all_to_all(grad_edge, "edge", split_axis=0, concat_axis=0, tiled=True)
    position = target_rows // edges_dev * span_rows + target_rows % span_rows
    grad_target = turned[position]
    return (hidden, grad_target)


def solution(mesh):
    placed = (
        P(("grp", "edge"), "feat"),
        P("feat", None),
        P(),
        P(None, "feat"),
        P(),
        P(("grp", "edge"), "rep", None, None),
        P("grp", None),
        P(("grp", "edge")),
        P(("grp", "edge"), "feat"),
    )
    return jax.shard_map(
        on_device,
        mesh=mesh,
        in_specs=placed,
        out_specs=(P(("grp", "edge"), "feat"), P(("grp", "edge"), "feat")),
        check_vma=False,
    )
```

profile of v0, /device:TPU:0, one launch (start us, length us, event | category | flops | bytes accessed | tf_op | source)
XLA Modules:
  0.0 345.4 jit_solution(14522135621438280731)
XLA Ops:
  7.2 2.2 fusion.52
  10.9 25.9 %all-reduce.5.cloned.1.call-done = f32[1024,64]{0,1:T(8,128)} async-done(((f32[1024,64]{0,1:T(8,128)}), f32[1024,64]{0,1:T(8,128)}) %all-reduce.5.cloned.1.call-update) | async-done | bytes 262160 | tf_op jit(solution)/shard_map/psum | solution.py:13
  37.8 2.1 gather_fusion
  39.9 4.6 %all-to-all-start = ((bf16[4,32,128,64]{2,3,1,0:T(8,128)(2,1)}), bf16[4,32,128,64]{2,3,1,0:T(8,128)(2,1)}, u32[]{:S(2)}, u32[]{:S(2)}) async-start(bf16[4,32,128,64]{2,3,1,0:T(8,128)(2,1)} %bitcast.124), calls=%async_computation | async-start | bytes 4194304 | tf_op jit(solution)/shard_map/all_to_all | solution.py:21
  44.8 47.7 %all-to-all-done = bf16[4,32,128,64]{2,3,1,0:T(8,128)(2,1)} async-done(((bf16[4,32,128,64]{2,3,1,0:T(8,128)(2,1)}), bf16[4,32,128,64]{2,3,1,0:T(8,128)(2,1)}, u32[]{:S(2)}, u32[]{:S(2)}) %all-to-all-start) | async-done | bytes 2097184 | tf_op jit(solution)/shard_map/all_to_all | solution.py:21
  92.5 2.4 gather_fusion.1
  95.8 4.2 %all-reduce.10 = bf16[1024,64]{0,1:T(8,128)(2,1)S(1)} all-reduce(f32[1024,64]{0,1:T(8,128)S(1)} %bitcast.129), channel_id=1, replica_groups=mesh['grp'=2,'edge'=4,'feat'=2,'rep'=2] {'rep'}, use_global_device_ids=true, to_apply=%region_4.5 | all-reduce | flops 65536 | bytes 393216 | tf_op jit(solution)/shard_map/psum | solution.py:17
  100.2 2.2 fusion
  104.6 17.4 %all-gather.5.cloned.1.call-done = bf16[1024,512]{1,0:T(8,128)(2,1)} async-done(((bf16[1024,256]{1,0:T(8,128)(2,1)}), bf16[1024,512]{1,0:T(8,128)(2,1)}) %all-gather.5.cloned.1.call-update) | async-done | bytes 1048592 | tf_op jit(solution)/shard_map/all_gather | solution.py:25
  122.0 2.8 add_convert_fusion.1
  124.9 21.4 %all-gather.7.cloned.1.call-done = bf16[1024,512]{1,0:T(8,128)(2,1)} async-done(((bf16[1024,256]{1,0:T(8,128)(2,1)}), bf16[1024,512]{1,0:T(8,128)(2,1)}) %all-gather.7.cloned.1.call-update) | async-done | bytes 1048592 | tf_op jit(solution)/shard_map/all_gather | solution.py:25
  146.3 3.3 fusion.4
  149.7 21.4 %all-gather.9.cloned.1.call-done = bf16[1024,512]{1,0:T(8,128)(2,1)} async-done(((bf16[1024,256]{1,0:T(8,128)(2,1)}), bf16[1024,512]{1,0:T(8,128)(2,1)}) %all-gather.9.cloned.1.call-update) | async-done | bytes 1048592 | tf_op jit(solution)/shard_map/all_gather | solution.py:25
  171.1 3.4 multiply_convert_fusion
  174.5 21.4 %all-gather.11.cloned.1.call-done = bf16[1024,512]{1,0:T(8,128)(2,1)} async-done(((bf16[1024,256]{1,0:T(8,128)(2,1)}), bf16[1024,512]{1,0:T(8,128)(2,1)}) %all-gather.11.cloned.1.call-update) | async-done | bytes 1048592 | tf_op jit(solution)/shard_map/all_gather | solution.py:25
  199.7 23.4 %all-reduce.7.cloned.1.call-done = f32[1024,64]{0,1:T(8,128)} async-done(((f32[1024,64]{0,1:T(8,128)}), f32[1024,64]{0,1:T(8,128)}) %all-reduce.7.cloned.1.call-update) | async-done | bytes 262160 | tf_op jit(solution)/shard_map/psum | solution.py:13
  226.6 8.9 %scatter_fusion = bf16[4,32,128,64]{2,3,1,0:T(8,128)(2,1)} fusion(bf16[4,32,128,64]{2,3,1,0:T(8,128)(2,1)} %broadcast_in_dim.18, s32[64]{0:T(128)S(1)} %get-tuple-element.2, bf16[64,128,64]{1,2,0:T(8,128)(2,1)S(1)} %bitcast.125), kind=kCustom, calls=%fused_computation.3 | custom fusion | bytes 3146240 | tf_op jit(solution)/shard_map/scatter | solution.py:108
  235.5 4.3 %copy.29 = bf16[4,32,128,64]{2,1,3,0:T(8,128)(2,1)} copy(bf16[4,32,128,64]{2,3,1,0:T(8,128)(2,1)} %scatter_fusion) | data formatting | bytes 4194304 | tf_op jit(solution)/shard_map/scatter | solution.py:108
  239.7 4.6 %all-to-all-start.1 = ((bf16[4,32,128,64]{2,1,3,0:T(8,128)(2,1)}), bf16[4,32,128,64]{2,1,3,0:T(8,128)(2,1)}, u32[]{:S(2)}, u32[]{:S(2)}) async-start(bf16[4,32,128,64]{2,1,3,0:T(8,128)(2,1)} %copy.29), calls=%async_computation.1 | async-start | bytes 4194304 | tf_op jit(solution)/shard_map/all_to_all | solution.py:21
  244.6 47.7 %all-to-all-done.1 = bf16[4,32,128,64]{2,1,3,0:T(8,128)(2,1)} async-done(((bf16[4,32,128,64]{2,1,3,0:T(8,128)(2,1)}), bf16[4,32,128,64]{2,1,3,0:T(8,128)(2,1)}, u32[]{:S(2)}, u32[]{:S(2)}) %all-to-all-start.1) | async-done | bytes 2097184 | tf_op jit(solution)/shard_map/all_to_all | solution.py:21
  295.1 16.6 %all-reduce.9.cloned.1.call-done = f32[1024,64]{0,1:T(8,128)} async-done(((f32[1024,64]{0,1:T(8,128)}), f32[1024,64]{0,1:T(8,128)}) %all-reduce.9.cloned.1.call-update) | async-done | bytes 262160 | tf_op jit(solution)/shard_map/psum | solution.py:17
  313.8 4.9 %all-to-all-start.2 = ((bf16[4,256,256]{2,1,0:T(8,128)(2,1)}), bf16[4,256,256]{2,1,0:T(8,128)(2,1)S(1)}, u32[]{:S(2)}, u32[]{:S(2)}) async-start(bf16[4,256,256]{2,1,0:T(8,128)(2,1)} %bitcast.22), calls=%async_computation.2 | async-start | bytes 1048576 | tf_op jit(solution)/shard_map/all_to_all | solution.py:125
  318.7 14.9 %all-to-all-done.2 = bf16[4,256,256]{2,1,0:T(8,128)(2,1)S(1)} async-done(((bf16[4,256,256]{2,1,0:T(8,128)(2,1)}), bf16[4,256,256]{2,1,0:T(8,128)(2,1)S(1)}, u32[]{:S(2)}, u32[]{:S(2)}) %all-to-all-start.2) | async-done | bytes 524320 | tf_op jit(solution)/shard_map/all_to_all | solution.py:125
  333.6 5.0 %gather_fusion.2 = bf16[1024,256]{1,0:T(8,128)(2,1)} fusion(bf16[1024,256]{1,0:T(8,128)(2,1)S(1)} %bitcast.123, s32[1024]{0:T(1024)S(1)} %fusion.33), kind=kCustom, calls=%fused_computation.2 | custom fusion | bytes 1052672 | tf_op jit(solution)/shard_map/gather | solution.py:127
  (66 shorter events, 18.7 us)
Async XLA Ops:
  7.2 87.7 %copy-start = (bf16[8,8,128,128]{3,2,1,0:T(8,128)(2,1)S(1)}, bf16[8,8,128,128]{3,2,1,0:T(8,128)(2,1)}, u32[]{:S(2)}) copy-start(bf16[8,8,128,128]{3,2,1,0:T(8,128)(2,1)} %param.14) | copy-start | bytes 6291460
  7.2 29.6 %all-reduce.5.cloned.1.call-start = ((), (), s32[]{:S(2)}) async-start(), calls=%async_computation.3 | async-start | bytes 524288 | tf_op jit(solution)/shard_map/psum | solution.py:13
  39.9 52.5 %all-to-all-start = ((bf16[4,32,128,64]{2,3,1,0:T(8,128)(2,1)}), bf16[4,32,128,64]{2,3,1,0:T(8,128)(2,1)}, u32[]{:S(2)}, u32[]{:S(2)}) async-start(bf16[4,32,128,64]{2,3,1,0:T(8,128)(2,1)} %bitcast.124), calls=%async_computation | async-start | bytes 4194304 | tf_op jit(solution)/shard_map/all_to_all | solution.py:21
  44.5 77.5 %all-gather.5.cloned.1.call-start = ((), (), s32[]{:S(2)}) async-start(), calls=%async_computation.4 | async-start | bytes 1572864 | tf_op jit(solution)/shard_map/all_gather | solution.py:25
  94.9 5.1 %copy-start.8 = (bf16[64,64]{1,0:T(8,128)(2,1)S(1)}, bf16[64,64]{1,0:T(8,128)(2,1)}, u32[]{:S(2)}) copy-start(bf16[64,64]{1,0:T(8,128)(2,1)} %param.11) | copy-start | bytes 24580
  94.9 5.3 %copy-start.6 = (bf16[64,256]{1,0:T(8,128)(2,1)S(1)}, bf16[64,256]{1,0:T(8,128)(2,1)}, u32[]{:S(2)}) copy-start(bf16[64,256]{1,0:T(8,128)(2,1)} %param.12) | copy-start | bytes 98308
  102.4 19.6 %copy-start.3 = (bf16[1024,256]{1,0:T(8,128)(2,1)S(1)}, bf16[1024,256]{1,0:T(8,128)(2,1)}, u32[]{:S(2)}) copy-start(bf16[1024,256]{1,0:T(8,128)(2,1)} %fusion) | copy-start | bytes 1572868
  102.4 43.9 %all-gather.7.cloned.1.call-start = ((), (), s32[]{:S(2)}) async-start(), calls=%async_computation.5 | async-start | bytes 1572864 | tf_op jit(solution)/shard_map/all_gather | solution.py:25
  124.9 46.2 %all-gather.9.cloned.1.call-start = ((), (), s32[]{:S(2)}) async-start(), calls=%async_computation.6 | async-start | bytes 1572864 | tf_op jit(solution)/shard_map/all_gather | solution.py:25
  146.3 24.8 %copy-start.4 = (bf16[1,512,512]{2,1,0:T(8,128)(2,1)S(1)}, bf16[1,512,512]{2,1,0:T(8,128)(2,1)}, u32[]{:S(2)}) copy-start(bf16[1,512,512]{2,1,0:T(8,128)(2,1)} %get-tuple-element.8) | copy-start | bytes 1572868
  149.6 46.3 %all-gather.11.cloned.1.call-start = ((), (), s32[]{:S(2)}) async-start(), calls=%async_computation.7 | async-start | bytes 1572864 | tf_op jit(solution)/shard_map/all_gather | solution.py:25
  174.5 48.6 %all-reduce.7.cloned.1.call-start = ((), (), s32[]{:S(2)}) async-start(), calls=%async_computation.8 | async-start | bytes 524288 | tf_op jit(solution)/shard_map/psum | solution.py:13
  197.9 0.8 copy-start.1
  239.7 52.5 %all-to-all-start.1 = ((bf16[4,32,128,64]{2,1,3,0:T(8,128)(2,1)}), bf16[4,32,128,64]{2,1,3,0:T(8,128)(2,1)}, u32[]{:S(2)}, u32[]{:S(2)}) async-start(bf16[4,32,128,64]{2,1,3,0:T(8,128)(2,1)} %copy.29), calls=%async_computation.1 | async-start | bytes 4194304 | tf_op jit(solution)/shard_map/all_to_all | solution.py:21
  244.3 67.4 %copy-start.2 = (bf16[1024,256]{1,0:T(8,128)(2,1)S(1)}, bf16[1024,256]{1,0:T(8,128)(2,1)}, u32[]{:S(2)}) copy-start(bf16[1024,256]{1,0:T(8,128)(2,1)} %copy-done.1) | copy-start | bytes 1572868
  244.3 67.4 %copy-start.5 = (f32[1024,64]{0,1:T(8,128)S(1)}, f32[1024,64]{0,1:T(8,128)}, u32[]{:S(2)}) copy-start(f32[1024,64]{0,1:T(8,128)} %all-reduce.5.cloned.1.call-done) | copy-start | bytes 786436
  244.3 67.4 %copy-start.7 = (bf16[256,64]{0,1:T(8,128)(2,1)S(1)}, bf16[256,64]{0,1:T(8,128)(2,1)}, u32[]{:S(2)}) copy-start(bf16[256,64]{0,1:T(8,128)(2,1)} %param.10) | copy-start | bytes 98308
  244.4 67.4 %all-reduce.9.cloned.1.call-start = ((), (), s32[]{:S(2)}) async-start(), calls=%async_computation.9 | async-start | bytes 524288 | tf_op jit(solution)/shard_map/psum | solution.py:17
  294.4 24.3 %copy-start.9 = (s32[1024]{0:T(1024)S(1)}, s32[1024]{0:T(1024)}, u32[]{:S(2)}) copy-start(s32[1024]{0:T(1024)} %param.16) | copy-start | bytes 12292
  313.8 19.8 %all-to-all-start.2 = ((bf16[4,256,256]{2,1,0:T(8,128)(2,1)}), bf16[4,256,256]{2,1,0:T(8,128)(2,1)S(1)}, u32[]{:S(2)}, u32[]{:S(2)}) async-start(bf16[4,256,256]{2,1,0:T(8,128)(2,1)} %bitcast.22), calls=%async_computation.2 | async-start | bytes 1048576 | tf_op jit(solution)/shard_map/all_to_all | solution.py:125
Sparse Core Ops, SparseCore 0:
  10.9 25.8 all-reduce.4
  102.5 19.4 all-gather.4
  125.0 21.2 all-gather.6
  149.8 21.2 all-gather.8
  174.6 21.2 all-gather.10
  199.8 23.1 all-reduce.6
  295.3 16.3 all-reduce.8
where the time goes:
time: 347 us; the launch traced here: 345 us
  waiting for transfers between devices  258 us (74%)
  local copies, waits for them, and re-layouts  29.2 us (8%)
  matrix products  23.7 us (7%)
  starting transfers between devices  14.3 us (4%)
  between operations  14.3 us (4%)
  blocking collectives  4.17 us (1%)
    all_to_all x2, waiting for transfers between devices, trade(): lax.all_to_all(payload, 'edge', split_axis=0, concat_axis=0, tiled=True)  95.4 us
    all_gather x4, waiting for transfers between devices, contract(): piece = lax.all_gather(values, 'feat', axis=1, tiled=True)  81.6 us
    psum x2, waiting for transfers between devices, feat_total(): return lax.psum(value, 'feat')  49.2 us
    psum x1, waiting for transfers between devices, rep_total(): return lax.psum(value, 'rep')  16.6 us
    all_to_all x1, waiting for transfers between devices, on_device(): lax.all_to_all(grad_edge, 'edge', split_axis=0, concat_axis=0, tiled=True)  14.9 us
    scatter x2, local copies, waits for them, and re-layouts, on_device(): outgoing = jnp.zeros((peers, capacity, block_rows, width_tri), jnp.bfloat...  13.1 us
    dot_general x4, matrix products, contract(): jnp.dot(piece, piece_weight(jnp.int32(0), piece.shape[1]), preferred_elem...  11.5 us
    all_to_all x2, starting transfers between devices, trade(): lax.all_to_all(payload, 'edge', split_axis=0, concat_axis=0, tiled=True)  9.2 us
  transfers between devices with their start and end apart: 10, of which 10 were waited for; matrix products, arithmetic and copies ran while one was open for 1% of the time, Pallas kernels for 0%

commit v1 on v0

--- a/solution.py
+++ b/solution.py
@@ -1,7 +1,507 @@
+import functools
+
 import jax
 import jax.numpy as jnp
 from jax import lax
+from jax.experimental import pallas as pl
+from jax.experimental.pallas import tpu as pltpu
 from jax.sharding import PartitionSpec as P
+
+MESH = pl.DeviceIdType.MESH
+F32 = jnp.float32
+BF16 = jnp.bfloat16
+
+
+def mm(a, b, ca, cb):
+    return lax.dot_general(a, b, (((ca,), (cb,)), ((), ())), preferred_element_type=F32)
+
+
+def slope(value):
+    sig = jax.nn.sigmoid(value)
+    return sig * (1.0 + value * (1.0 - sig))
+
+
+def block_kernel(
+    n_edge,
+    source,
+    links,
+    wanted,
+    w_bil,
+    edge_hbm,
+    down_hbm,
+    up_hbm,
+    res_hbm,
+    coef_hbm,
+    cot_hbm,
+    edge_out,
+    grad_out,
+    emb,
+    cot,
+    w_down,
+    w_up,
+    w_res,
+    coef,
+    down_mine,
+    table,
+    tri_part,
+    tri_in,
+    bil_mine,
+    grad_tri,
+    chain,
+    pair_out,
+    pair_in,
+    red_out,
+    red_in,
+    out_mine,
+    ge,
+    turned,
+    grad_v,
+    local_sem,
+    x_send,
+    x_recv,
+    tab_send,
+    tab_recv,
+    core_send,
+    core_recv,
+    tri_send,
+    tri_recv,
+    bil_send,
+    bil_recv,
+    pair_send,
+    pair_recv,
+    red_send,
+    red_recv,
+    out_send,
+    out_recv,
+    ge_send,
+    ge_recv,
+    fin_send,
+    fin_recv,
+    fin_local,
+):
+    g = lax.axis_index("grp")
+    e = lax.axis_index("edge")
+    f = lax.axis_index("feat")
+    r = lax.axis_index("rep")
+    of = 1 - f
+    orr = 1 - r
+    s = 2 * f + r
+    blocks, tiles, rows_b, _ = coef.shape
+    bpd = blocks // 4
+    rows = emb.shape[1]
+    half_c = table.shape[1]
+    span = turned.shape[0] // n_edge
+    spd = rows // span
+    hs = span // 2
+
+    def peer(d, df, dr):
+        return (g, lax.rem(e + d, n_edge), of if df else f, orr if dr else r)
+
+    def remote(src, dst, ss, rs, dev):
+        return pltpu.make_async_remote_copy(
+            src_ref=src, dst_ref=dst, send_sem=ss, recv_sem=rs, device_id=dev, device_id_type=MESH
+        )
+
+    def mine(who):
+        return pl.ds(who * rows, rows)
+
+    local = [
+        pltpu.make_async_copy(down_hbm, w_down.at[f], local_sem.at[0]),
+        pltpu.make_async_copy(edge_hbm.at[mine(s)], emb.at[f], local_sem.at[1]),
+        pltpu.make_async_copy(up_hbm, w_up.at[f], local_sem.at[2]),
+        pltpu.make_async_copy(coef_hbm, coef, local_sem.at[3]),
+        pltpu.make_async_copy(res_hbm, w_res, local_sem.at[4]),
+        pltpu.make_async_copy(cot_hbm.at[mine(s)], cot.at[f], local_sem.at[5]),
+    ]
+    for copy in local:
+        copy.start()
+
+    barrier = pltpu.get_barrier_semaphore()
+    others = 0
+    for d in range(n_edge):
+        for df in range(2):
+            for dr in range(2):
+                if d or df or dr:
+                    pl.semaphore_signal(
+                        barrier, inc=1, device_id=peer(d, df, dr), device_id_type=MESH
+                    )
+                    others += 1
+    pl.semaphore_wait(barrier, others)
+
+    across = peer(0, 1, 0)
+    partner_rows = mine(2 * of + r)
+    xs = [
+        remote(down_hbm, w_down.at[f], x_send.at[0], x_recv.at[0], across),
+        remote(edge_hbm.at[partner_rows], emb.at[f], x_send.at[1], x_recv.at[1], across),
+        remote(up_hbm, w_up.at[f], x_send.at[2], x_recv.at[2], across),
+        remote(cot_hbm.at[partner_rows], cot.at[f], x_send.at[3], x_recv.at[3], across),
+    ]
+    for copy in xs:
+        copy.start()
+    local[0].wait()
+    local[1].wait()
+    xs[0].wait_recv()
+    xs[1].wait_recv()
+    embed = jnp.concatenate([emb[0], emb[1]], axis=1)
+    wd = jnp.concatenate([w_down[0], w_down[1]], axis=0)
+    pre_down = mm(wd, embed, 0, 1)
+    down = jax.nn.silu(pre_down).astype(BF16)
+    for h in range(2):
+        for b in range(bpd):
+            down_mine[h, b] = down[h * half_c : (h + 1) * half_c, b * rows_b : (b + 1) * rows_b]
+
+    def region(ed, who):
+        return pl.ds(ed * blocks + who * bpd, bpd)
+
+    tabs = []
+    for i in range(1, 2 * n_edge):
+        d, df = i // 2, i % 2
+        copy = remote(
+            down_mine.at[of if df else f],
+            table.at[region(e, s)],
+            tab_send.at[i],
+            tab_recv.at[i],
+            peer(d, df, 0),
+        )
+        copy.start()
+        tabs.append(copy)
+    own = remote(
+        down_mine.at[f], table.at[region(e, s)], core_send.at[0], core_recv.at[0], peer(0, 0, 1)
+    )
+    own.start()
+    table[region(e, s)] = down_mine[f]
+    cores = [own]
+    for i in range(1, 2 * n_edge):
+        d, df = i // 2, i % 2
+        tabs[i - 1].wait_recv()
+        place = region(lax.rem(e + n_edge - d, n_edge), 2 * (of if df else f) + r)
+        copy = remote(
+            table.at[place], table.at[place], core_send.at[i], core_recv.at[i], peer(0, 0, 1)
+        )
+        copy.start()
+        cores.append(copy)
+    local[3].wait()
+    for copy in cores:
+        copy.wait_recv()
+
+    def forward(n, _):
+        total = jnp.zeros((half_c, rows_b), F32)
+        for k in range(tiles):
+            total += mm(table[source[e * blocks + n, r * tiles + k]], coef[n, k], 1, 1)
+        tri_part[n] = total
+        return 0
+
+    lax.fori_loop(0, blocks, forward, 0)
+    tris = []
+    for i in range(1, 4):
+        df, dr = i // 2, i % 2
+        to = 2 * (of if df else f) + (orr if dr else r)
+        copy = remote(
+            tri_part.at[pl.ds(to * bpd, bpd)],
+            tri_in.at[i],
+            tri_send.at[i],
+            tri_recv.at[i],
+            peer(0, df, dr),
+        )
+        copy.start()
+        tris.append(copy)
+    for copy in tris:
+        copy.wait_recv()
+    near = tri_part[pl.ds(s * bpd, bpd)] + tri_in[1]
+    far = tri_in[2] + tri_in[3]
+    low = jnp.where(f == 0, near, far)
+    high = jnp.where(f == 0, far, near)
+    tri = jnp.concatenate(
+        [jnp.concatenate([low[b], high[b]], axis=0) for b in range(bpd)], axis=1
+    ).astype(BF16)
+    wb = w_bil[...]
+    pre_bil = mm(wb, tri, 0, 0)
+    mid = jax.nn.silu(pre_bil).astype(BF16)
+    local[2].wait()
+    xs[2].wait_recv()
+    wu = jnp.concatenate([w_up[0], w_up[1]], axis=1)
+    hidden = (embed.astype(F32) + mm(mid, wu, 0, 0)).astype(BF16)
+    local[4].wait()
+    saved = []
+    for layer in range(w_res.shape[0]):
+        pre = mm(hidden, w_res[layer], 1, 0)
+        hidden = (hidden.astype(F32) + jax.nn.silu(pre)).astype(BF16)
+        saved.append(slope(pre))
+    cols = emb.shape[2]
+    for h in range(2):
+        out_mine[h] = hidden[:, h * cols : (h + 1) * cols]
+    outs = []
+    for i in range(1, 4):
+        df, dr = i // 2, i % 2
+        copy = remote(
+            out_mine.at[of if df else f],
+            edge_out.at[mine(s)],
+            out_send.at[i],
+            out_recv.at[i],
+            peer(0, df, dr),
+        )
+        outs.append(copy)
+    out_local = pltpu.make_async_copy(out_mine.at[f], edge_out.at[mine(s)], local_sem.at[6])
+    out_local.start()
+    local[5].wait()
+    xs[3].wait_recv()
+    grad = jnp.concatenate([cot[0], cot[1]], axis=1).astype(F32)
+    for layer in range(w_res.shape[0] - 1, -1, -1):
+        dz = (grad * saved[layer]).astype(BF16)
+        grad = grad + mm(dz, w_res[layer], 1, 1)
+    grad_hb = grad.astype(BF16)
+    grad_bil = (mm(wu, grad_hb, 1, 1) * slope(pre_bil)).astype(BF16)
+    grad_t = mm(wb, grad_bil, 1, 0).astype(BF16)
+    for h in range(2):
+        for b in range(bpd):
+            bil_mine[h, b] = grad_t[h * half_c : (h + 1) * half_c, b * rows_b : (b + 1) * rows_b]
+    bils = []
+    for i in range(1, 4):
+        df, dr = i // 2, i % 2
+        copy = remote(
+            bil_mine.at[of if df else f],
+            grad_tri.at[pl.ds(s * bpd, bpd)],
+            bil_send.at[i],
+            bil_recv.at[i],
+            peer(0, df, dr),
+        )
+        copy.start()
+        bils.append(copy)
+    for copy in outs:
+        copy.start()
+    grad_tri[pl.ds(s * bpd, bpd)] = bil_mine[f]
+    chain[0] = jnp.zeros((half_c, rows_b), F32)
+    for copy in bils:
+        copy.wait_recv()
+
+    def backward(n, _):
+        block = grad_tri[n]
+        parts = [mm(block, coef[n, k], 1, 0) for k in range(tiles)]
+        for k in range(tiles):
+            t = n * tiles + k
+            chain[t + 1] = parts[k] + chain[links[t]]
+        return 0
+
+    lax.fori_loop(0, blocks, backward, 0)
+    entries = blocks * tiles
+    for i in range(2 * n_edge):
+        for b in range(bpd):
+            block_id = (i // 2) * blocks + (2 * (i % 2) + orr) * bpd + b
+            pair_out[i, b] = chain[links[entries + block_id]]
+    pair = remote(pair_out, pair_in, pair_send, pair_recv, peer(0, 0, 1))
+    pair.start()
+    pair.wait_recv()
+    for i in range(2 * n_edge):
+        for b in range(bpd):
+            block_id = (i // 2) * blocks + (2 * (i % 2) + r) * bpd + b
+            red_out[i, b] = (chain[links[entries + block_id]] + pair_in[i, b]).astype(BF16)
+    reds = []
+    for i in range(1, 2 * n_edge):
+        d, df = i // 2, i % 2
+        slot = 2 * lax.rem(e + d, n_edge) + (of if df else f)
+        copy = remote(
+            red_out.at[slot], red_in.at[i], red_send.at[i], red_recv.at[i], peer(d, df, 0)
+        )
+        copy.start()
+        reds.append(copy)
+    for copy in reds:
+        copy.wait_recv()
+    near = red_out[2 * e + f].astype(F32)
+    far = red_in[1].astype(F32)
+    for d in range(1, n_edge):
+        near += red_in[2 * d].astype(F32)
+        far += red_in[2 * d + 1].astype(F32)
+    low = jnp.where(f == 0, near, far)
+    high = jnp.where(f == 0, far, near)
+    grad_down = jnp.concatenate(
+        [jnp.concatenate([low[b], high[b]], axis=0) for b in range(bpd)], axis=1
+    )
+    grad_pre = (grad_down * slope(pre_down)).astype(BF16)
+    grad_edge = (grad_hb.astype(F32) + mm(grad_pre, wd, 0, 1)).astype(BF16)
+    for h in range(2):
+        ge[h] = grad_edge[:, h * cols : (h + 1) * cols]
+
+    sends = []
+    for j in range(spd):
+        q = s * spd + j
+        d = lax.rem(q - e + n_edge, n_edge)
+        for df in range(2):
+            for dr in range(2):
+                rt = orr if dr else r
+                fr = of if df else f
+                src = ge.at[fr, pl.ds(j * span + rt * hs, hs)]
+                dst = turned.at[pl.ds(e * span + rt * hs, hs)]
+                copy = remote(
+                    src,
+                    dst,
+                    ge_send.at[j, 2 * df + dr],
+                    ge_recv.at[d],
+                    (g, q, fr, rt),
+                )
+                if df or dr:
+                    copy.start()
+                    sends.append((copy, None))
+                else:
+                    keep = pltpu.make_async_copy(src, dst, fin_local)
+
+                    @pl.when(q == e)
+                    def _(keep=keep):
+                        keep.start()
+                        keep.wait()
+
+                    @pl.when(q != e)
+                    def _(copy=copy):
+                        copy.start()
+
+                    sends.append((copy, q != e))
+    fins = []
+    for d in range(n_edge):
+        p = lax.rem(e + n_edge - d, n_edge)
+        place = pl.ds(p * span + r * hs, hs)
+        arrive = remote(
+            turned.at[place], turned.at[place], ge_send.at[0, 0], ge_recv.at[d], peer(0, 0, 1)
+        )
+        if d:
+            arrive.wait_recv()
+        else:
+
+            @pl.when(s != e // spd)
+            def _(arrive=arrive):
+                arrive.wait_recv()
+
+        copy = remote(
+            turned.at[place], turned.at[place], fin_send.at[d], fin_recv.at[d], peer(0, 0, 1)
+        )
+        copy.start()
+        fins.append(copy)
+    writes = []
+    for d in range(n_edge):
+        p = lax.rem(e + n_edge - d, n_edge)
+        fins[d].wait_recv()
+        wish = wanted[p]
+        slot = lax.broadcasted_iota(jnp.int32, (span, span), 0)
+        pick = jnp.where(slot == wish, 1.0, 0.0).astype(BF16)
+        place = pl.ds(p * span, span)
+        grad_v[place] = mm(pick, turned[place], 0, 0).astype(BF16)
+        copy = pltpu.make_async_copy(grad_v.at[place], grad_out.at[place], local_sem.at[7 + d])
+        copy.start()
+        writes.append(copy)
+    for copy in outs:
+        copy.wait()
+    out_local.wait()
+    for copy in xs + tabs + cores + tris + bils + [pair] + reds + fins:
+        copy.wait_send()
+    for copy, when in sends:
+        if when is None:
+            copy.wait_send()
+        else:
+
+            @pl.when(when)
+            def _(copy=copy):
+                copy.wait_send()
+
+    for copy in writes:
+        copy.wait()
+
+
+def fused(
+    edge_embed, w_down, w_bilinear, w_up, w_residual, tile_coef, tile_source, target_rows, cotangent
+):
+    n_edge = lax.axis_size("edge")
+    edges, cols = edge_embed.shape
+    blocks, tiles, rows_b, _ = tile_coef.shape
+    width = w_down.shape[1]
+    half_c = width // 2
+    bpd = blocks // 4
+    rows = edges // 4
+    span = edges // n_edge
+    n_blocks = n_edge * blocks
+    entries = blocks * tiles
+    mine = lax.dynamic_slice(
+        tile_source,
+        (lax.axis_index("edge") * blocks, lax.axis_index("rep") * tiles),
+        (blocks, tiles),
+    ).reshape(entries)
+    asked = jnp.concatenate([mine, jnp.arange(n_blocks, dtype=jnp.int32)])
+    before = jnp.concatenate(
+        [jnp.arange(entries, dtype=jnp.int32), jnp.full((n_blocks,), entries, jnp.int32)]
+    )
+    order = jnp.arange(entries, dtype=jnp.int32)
+    same = (asked[:, None] == mine[None, :]) & (order[None, :] < before[:, None])
+    links = jnp.max(jnp.where(same, order[None, :] + 1, 0), axis=1)
+    wanted = (target_rows % span).reshape(n_edge, 1, span)
+    vmem = pl.BlockSpec(memory_space=pltpu.VMEM)
+    smem = pl.BlockSpec(memory_space=pltpu.SMEM)
+    hbm = pl.BlockSpec(memory_space=pl.ANY)
+    dma = pltpu.SemaphoreType.DMA
+    tile = (bpd, half_c, rows_b)
+    n2 = 2 * n_edge
+    return pl.pallas_call(
+        functools.partial(block_kernel, n_edge),
+        out_shape=[jax.ShapeDtypeStruct((edges, cols), BF16)] * 2,
+        in_specs=[smem, smem, vmem, vmem] + [hbm] * 6,
+        out_specs=[hbm, hbm],
+        scratch_shapes=[
+            pltpu.VMEM((2, rows, cols), BF16),
+            pltpu.VMEM((2, rows, cols), BF16),
+            pltpu.VMEM((2,) + w_down.shape, BF16),
+            pltpu.VMEM((2,) + w_up.shape, BF16),
+            pltpu.VMEM(w_residual.shape, BF16),
+            pltpu.VMEM(tile_coef.shape, BF16),
+            pltpu.VMEM((2,) + tile, BF16),
+            pltpu.VMEM((n_blocks, half_c, rows_b), BF16),
+            pltpu.VMEM((blocks, half_c, rows_b), F32),
+            pltpu.VMEM((4,) + tile, F32),
+            pltpu.VMEM((2,) + tile, BF16),
+            pltpu.VMEM((blocks, half_c, rows_b), BF16),
+            pltpu.VMEM((entries + 1, half_c, rows_b), F32),
+            pltpu.VMEM((n2,) + tile, F32),
+            pltpu.VMEM((n2,) + tile, F32),
+            pltpu.VMEM((n2,) + tile, BF16),
+            pltpu.VMEM((n2,) + tile, BF16),
+            pltpu.VMEM((2, rows, cols), BF16),
+            pltpu.VMEM((2, rows, cols), BF16),
+            pltpu.VMEM((edges, cols), BF16),
+            pltpu.VMEM((edges, cols), BF16),
+            dma((7 + n_edge,)),
+            dma((4,)),
+            dma((4,)),
+            dma((n2,)),
+            dma((n2,)),
+            dma((n2,)),
+            dma((n2,)),
+            dma((4,)),
+            dma((4,)),
+            dma((4,)),
+            dma((4,)),
+            dma(()),
+            dma(()),
+            dma((n2,)),
+            dma((n2,)),
+            dma((4,)),
+            dma((4,)),
+            dma((rows // span, 4)),
+            dma((n_edge,)),
+            dma((n_edge,)),
+            dma((n_edge,)),
+            dma(()),
+        ],
+        compiler_params=pltpu.CompilerParams(
+            collective_id=0, has_side_effects=True, vmem_limit_bytes=40 * 1024 * 1024
+        ),
+        name="interaction",
+    )(
+        tile_source,
+        links,
+        wanted,
+        w_bilinear,
+        edge_embed,
+        w_down,
+        w_up,
+        w_residual,
+        tile_coef,
+        cotangent,
+    )
 
 
 def silu_slope(value):
@@ -140,8 +640,9 @@
         P(("grp", "edge")),
         P(("grp", "edge"), "feat"),
     )
+    fits = mesh.shape["feat"] == 2 and mesh.shape["rep"] == 2
     return jax.shard_map(
-        on_device,
+        fused if fits else on_device,
         mesh=mesh,
         in_specs=placed,
         out_specs=(P(("grp", "edge"), "feat"), P(("grp", "edge"), "feat")),

time: 347 us -> 65.8 us (0.19)
  waiting for transfers between devices: 258 us -> 0 us
  Pallas kernels: 0 us -> 51.8 us
  matrix products: 23.7 us -> 0 us
  local copies, waits for them, and re-layouts: 29.2 us -> 10.5 us
  starting transfers between devices: 14.3 us -> 0 us
  between operations: 14.3 us -> 0.68 us
  blocking collectives: 4.17 us -> 0 us
    all_to_all x3 -> x0, waiting for transfers between devices: 110 us -> none  [the longest x2 95.4 us: trade(): lax.all_to_all(payload, 'edge', split_axis=0, concat_axis=0, tiled=True)]
    all_gather x4 -> x0, waiting for transfers between devices: 81.6 us -> none  [contract(): piece = lax.all_gather(values, 'feat', axis=1, tiled=True)]
    psum x3 -> x0, waiting for transfers between devices: 65.8 us -> none  [the longest x2 49.2 us: feat_total(): return lax.psum(value, 'feat')]
    pallas_call x0 -> x1, Pallas kernels: none -> 51.8 us  [fused(): pl.pallas_call(functools.partial(block_kernel, n_edge), out_shape=[jax.Sh...]
    dot_general x13 -> x0, matrix products: 23.7 us -> none  [the longest x4 11.5 us: contract(): jnp.dot(piece, piece_weight(jnp.int32(0), piece.shape[1]), preferred_elem...]
    all_to_all x3 -> x0, starting transfers between devices: 14.1 us -> none  [the longest x2 9.2 us: trade(): lax.all_to_all(payload, 'edge', split_axis=0, concat_axis=0, tiled=True)]
    scatter x2 -> x0, local copies, waits for them, and re-layouts: 13.1 us -> none  [on_device(): outgoing = jnp.zeros((peers, capacity, block_rows, width_tri), jnp.bfloat...]
    gather x3 -> x0, local copies, waits for them, and re-layouts: 9.5 us -> none  [the longest x1 4.98 us: on_device(): grad_target = turned[position]]
  transfers between devices with their start and end apart: 10 -> 0, of which waited for: 10 -> 0; matrix products, arithmetic and copies ran while one was open for 1% -> 0% of each run, Pallas kernels for 0% -> 0%
where the time goes in v1:
time: 65.8 us; the launch traced here: 64.6 us
  Pallas kernels  51.8 us (79%)
  local copies, waits for them, and re-layouts  10.5 us (16%)
  other arithmetic  1.53 us (2%)
  between operations  0.68 us (1%)
    pallas_call x1, Pallas kernels, fused(): pl.pallas_call(functools.partial(block_kernel, n_edge), out_shape=[jax.Sh...  51.8 us
    unnamed x16, local copies, waits for them, and re-layouts  9.6 us

profile of v1, /device:TPU:0, one launch (start us, length us, event | category | flops | bytes accessed | tf_op | source)
XLA Modules:
  0.0 64.6 jit_solution(14375690086886423548)
XLA Ops:
  0.7 0.8 %dynamic_slice.3 = s32[8,8]{0,1:T(8,128)S(1)} dynamic-slice(s32[32,16]{0,1:T(8,128)} %param.15, s32[]{:T(128)S(6)} %select_n.17, s32[]{:T(128)S(6)} %select_n.18), dynamic_slice_sizes={8,8} | dynamic-slice | bytes 516 | tf_op jit(solution)/shard_map/dynamic_slice | solution.py:420
  1.4 0.1 copy.14
  1.5 0.1 reshape.18
  1.6 0.1 pad_add_fusion
  1.7 0.8 %select_reduce_fusion.links = s32[96]{0:T(128)S(1)} fusion(s32[64]{0:T(128)S(1)} %iota_add_fusion, s32[96]{0:T(128)} %constant.33.clone.1, s32[96]{0:T(128)S(1)} %pad_add_fusion, s32[64]{0:T(128)S(1)} %reshape.18), kind=kLoop, calls=%fused_computation | loop fusion | flops 30624 | bytes 1664 | tf_op jit(solution)/shard_map/reduce_max | solution.py:431
  2.4 0.7 %add_select_fusion = s32[1024]{0:T(1024)S(1)} fusion(s32[1024]{0:T(1024)} %param.16), kind=kLoop, calls=%fused_computation.3 | loop fusion | flops 11264 | bytes 8192 | tf_op jit(solution)/shard_map/jit(remainder)/select_n | solution.py:432
  3.1 0.8 %copy.15.source = s32[32,16]{1,0:T(8,128)S(1)} copy(s32[32,16]{0,1:T(8,128)} %param.15) | data formatting | bytes 4096 | tf_op args[6]
  3.9 0.9 %copy.16.down_hbm = bf16[256,64]{1,0:T(8,128)(2,1)S(1)} copy(bf16[256,64]{0,1:T(8,128)(2,1)} %param.10) | data formatting | bytes 65536 | tf_op args[1]
  4.8 0.0 copy-start
  4.8 1.6 %copy-done = bf16[8,8,128,128]{3,2,1,0:T(8,128)(2,1)S(1)} copy-done((bf16[8,8,128,128]{3,2,1,0:T(8,128)(2,1)S(1)}, bf16[8,8,128,128]{3,2,1,0:T(8,128)(2,1)}, u32[]{:S(2)}) %copy-start) | copy-done | bytes 2097176
  6.4 0.0 copy-start.1
  6.4 1.2 %copy-done.1 = bf16[2,512,512]{2,1,0:T(8,128)(2,1)S(1)} copy-done((bf16[2,512,512]{2,1,0:T(8,128)(2,1)S(1)}, bf16[2,512,512]{2,1,0:T(8,128)(2,1)}, u32[]{:S(2)}) %copy-start.1) | copy-done | bytes 1048600
  7.6 0.0 copy-start.2
  7.6 1.0 %copy-done.2 = bf16[1024,256]{1,0:T(8,128)(2,1)S(1)} copy-done((bf16[1024,256]{1,0:T(8,128)(2,1)S(1)}, bf16[1024,256]{1,0:T(8,128)(2,1)}, u32[]{:S(2)}) %copy-start.2) | copy-done | bytes 524312
  8.6 0.0 copy-start.3
  8.6 1.0 %copy-done.3 = bf16[1024,256]{1,0:T(8,128)(2,1)S(1)} copy-done((bf16[1024,256]{1,0:T(8,128)(2,1)S(1)}, bf16[1024,256]{1,0:T(8,128)(2,1)}, u32[]{:S(2)}) %copy-start.3) | copy-done | bytes 524312
  9.7 0.0 copy-start.4
  9.7 0.8 %copy-done.4 = bf16[64,256]{1,0:T(8,128)(2,1)S(1)} copy-done((bf16[64,256]{1,0:T(8,128)(2,1)S(1)}, bf16[64,256]{1,0:T(8,128)(2,1)}, u32[]{:S(2)}) %copy-start.4) | copy-done | bytes 32792
  10.4 0.0 copy-start.5
  10.4 0.7 %copy-done.5 = bf16[64,64]{1,0:T(8,128)(2,1)S(1)} copy-done((bf16[64,64]{1,0:T(8,128)(2,1)S(1)}, bf16[64,64]{1,0:T(8,128)(2,1)}, u32[]{:S(2)}) %copy-start.5) | copy-done | bytes 8216
  11.1 51.8 %interaction.1 = (bf16[1024,256]{1,0:T(8,128)(2,1)S(1)}, bf16[1024,256]{1,0:T(8,128)(2,1)S(1)}) custom-call(s32[32,16]{1,0:T(8,128)S(1)} %copy.15.source, s32[96]{0:T(128)S(1)} %select_reduce_fusion.links, s32[4,1,256]{2,1,0:T(1,128)S(1)} %bitcast.1, bf16[64,64]{1,0:T(8,128)(2,1)S(1)} %copy-done.5, bf16[1024,256]{1,0:T(8,128)(2,1)S(1)} %copy-done.2, ...), custom_call_target="tpu_custom_call" | custom-call | tf_op jit(solution)/shard_map/interaction/pallas_call | solution.py:439
  63.0 0.8 %copy.19 = bf16[1024,256]{1,0:T(8,128)(2,1)} copy(bf16[1024,256]{1,0:T(8,128)(2,1)S(1)} %get-tuple-element.4) | data formatting | bytes 1048576
  63.8 0.8 %copy.20 = bf16[1024,256]{1,0:T(8,128)(2,1)} copy(bf16[1024,256]{1,0:T(8,128)(2,1)S(1)} %get-tuple-element.5) | data formatting | bytes 1048576
  (2 shorter events, 0.0 us)
Async XLA Ops:
  4.8 1.6 %copy-start = (bf16[8,8,128,128]{3,2,1,0:T(8,128)(2,1)S(1)}, bf16[8,8,128,128]{3,2,1,0:T(8,128)(2,1)}, u32[]{:S(2)}) copy-start(bf16[8,8,128,128]{3,2,1,0:T(8,128)(2,1)} %coef_hbm.1) | copy-start | bytes 6291460
  6.4 1.2 %copy-start.1 = (bf16[2,512,512]{2,1,0:T(8,128)(2,1)S(1)}, bf16[2,512,512]{2,1,0:T(8,128)(2,1)}, u32[]{:S(2)}) copy-start(bf16[2,512,512]{2,1,0:T(8,128)(2,1)} %res_hbm.1) | copy-start | bytes 3145732
  7.6 1.0 %copy-start.2 = (bf16[1024,256]{1,0:T(8,128)(2,1)S(1)}, bf16[1024,256]{1,0:T(8,128)(2,1)}, u32[]{:S(2)}) copy-start(bf16[1024,256]{1,0:T(8,128)(2,1)} %edge_hbm.1) | copy-start | bytes 1572868
  8.6 1.0 %copy-start.3 = (bf16[1024,256]{1,0:T(8,128)(2,1)S(1)}, bf16[1024,256]{1,0:T(8,128)(2,1)}, u32[]{:S(2)}) copy-start(bf16[1024,256]{1,0:T(8,128)(2,1)} %cot_hbm.1) | copy-start | bytes 1572868
  9.7 0.8 %copy-start.4 = (bf16[64,256]{1,0:T(8,128)(2,1)S(1)}, bf16[64,256]{1,0:T(8,128)(2,1)}, u32[]{:S(2)}) copy-start(bf16[64,256]{1,0:T(8,128)(2,1)} %up_hbm.1) | copy-start | bytes 98308
  10.4 0.7 %copy-start.5 = (bf16[64,64]{1,0:T(8,128)(2,1)S(1)}, bf16[64,64]{1,0:T(8,128)(2,1)}, u32[]{:S(2)}) copy-start(bf16[64,64]{1,0:T(8,128)(2,1)} %w_bil.1) | copy-start | bytes 24580

commit v2 on v1

--- a/solution.py
+++ b/solution.py
@@ -25,8 +25,8 @@
     n_edge,
     source,
     links,
-    wanted,
-    w_bil,
+    wanted_hbm,
+    bil_hbm,
     edge_hbm,
     down_hbm,
     up_hbm,
@@ -36,7 +36,12 @@
     edge_out,
     grad_out,
     emb,
+    emb_x,
+    pd_part,
+    pd_in,
     cot,
+    wanted,
+    w_bil,
     w_down,
     w_up,
     w_res,
@@ -55,6 +60,10 @@
     out_mine,
     ge,
     turned,
+    picks,
+    hb_perm,
+    gp_mine,
+    gp_in,
     grad_v,
     local_sem,
     x_send,
@@ -78,6 +87,8 @@
     fin_send,
     fin_recv,
     fin_local,
+    gp_send,
+    gp_recv,
 ):
     g = lax.axis_index("grp")
     e = lax.axis_index("edge")
@@ -105,13 +116,17 @@
     def mine(who):
         return pl.ds(who * rows, rows)
 
+    partner_rows = mine(2 * of + r)
     local = [
-        pltpu.make_async_copy(down_hbm, w_down.at[f], local_sem.at[0]),
+        pltpu.make_async_copy(down_hbm, w_down, local_sem.at[0]),
         pltpu.make_async_copy(edge_hbm.at[mine(s)], emb.at[f], local_sem.at[1]),
         pltpu.make_async_copy(up_hbm, w_up.at[f], local_sem.at[2]),
         pltpu.make_async_copy(coef_hbm, coef, local_sem.at[3]),
         pltpu.make_async_copy(res_hbm, w_res, local_sem.at[4]),
         pltpu.make_async_copy(cot_hbm.at[mine(s)], cot.at[f], local_sem.at[5]),
+        pltpu.make_async_copy(bil_hbm, w_bil, local_sem.at[7]),
+        pltpu.make_async_copy(wanted_hbm, wanted, local_sem.at[8]),
+        pltpu.make_async_copy(edge_hbm.at[partner_rows], emb_x, local_sem.at[9]),
     ]
     for copy in local:
         copy.start()
@@ -126,25 +141,24 @@
                         barrier, inc=1, device_id=peer(d, df, dr), device_id_type=MESH
                     )
                     others += 1
+    local[0].wait()
+    local[1].wait()
+    local[8].wait()
+    wd = w_down[...]
+    pd_part[...] = mm(wd, emb_x[...], 1, 1)
+    own_part = mm(wd, emb[f], 1, 1)
     pl.semaphore_wait(barrier, others)
 
     across = peer(0, 1, 0)
-    partner_rows = mine(2 * of + r)
     xs = [
-        remote(down_hbm, w_down.at[f], x_send.at[0], x_recv.at[0], across),
-        remote(edge_hbm.at[partner_rows], emb.at[f], x_send.at[1], x_recv.at[1], across),
+        remote(pd_part, pd_in, x_send.at[0], x_recv.at[0], across),
+        remote(emb_x, emb.at[f], x_send.at[1], x_recv.at[1], across),
         remote(up_hbm, w_up.at[f], x_send.at[2], x_recv.at[2], across),
         remote(cot_hbm.at[partner_rows], cot.at[f], x_send.at[3], x_recv.at[3], across),
     ]
-    for copy in xs:
-        copy.start()
-    local[0].wait()
-    local[1].wait()
+    xs[0].start()
     xs[0].wait_recv()
-    xs[1].wait_recv()
-    embed = jnp.concatenate([emb[0], emb[1]], axis=1)
-    wd = jnp.concatenate([w_down[0], w_down[1]], axis=0)
-    pre_down = mm(wd, embed, 0, 1)
+    pre_down = own_part + pd_in[...]
     down = jax.nn.silu(pre_down).astype(BF16)
     for h in range(2):
         for b in range(bpd):
@@ -169,6 +183,8 @@
         down_mine.at[f], table.at[region(e, s)], core_send.at[0], core_recv.at[0], peer(0, 0, 1)
     )
     own.start()
+    xs[1].start()
+    xs[2].start()
     table[region(e, s)] = down_mine[f]
     cores = [own]
     for i in range(1, 2 * n_edge):
@@ -184,10 +200,12 @@
     for copy in cores:
         copy.wait_recv()
 
+    xs[3].start()
+
     def forward(n, _):
         total = jnp.zeros((half_c, rows_b), F32)
         for k in range(tiles):
-            total += mm(table[source[e * blocks + n, r * tiles + k]], coef[n, k], 1, 1)
+            total += mm(table[source[r * tiles + k, e * blocks + n]], coef[n, k], 1, 1)
         tri_part[n] = total
         return 0
 
@@ -214,11 +232,14 @@
     tri = jnp.concatenate(
         [jnp.concatenate([low[b], high[b]], axis=0) for b in range(bpd)], axis=1
     ).astype(BF16)
+    local[6].wait()
     wb = w_bil[...]
     pre_bil = mm(wb, tri, 0, 0)
     mid = jax.nn.silu(pre_bil).astype(BF16)
     local[2].wait()
     xs[2].wait_recv()
+    xs[1].wait_recv()
+    embed = jnp.concatenate([emb[0], emb[1]], axis=1)
     wu = jnp.concatenate([w_up[0], w_up[1]], axis=1)
     hidden = (embed.astype(F32) + mm(mid, wu, 0, 0)).astype(BF16)
     local[4].wait()
@@ -231,15 +252,15 @@
     for h in range(2):
         out_mine[h] = hidden[:, h * cols : (h + 1) * cols]
     outs = []
-    for i in range(1, 4):
-        df, dr = i // 2, i % 2
+    for i in range(1, 3):
         copy = remote(
-            out_mine.at[of if df else f],
+            out_mine.at[of if i == 2 else f],
             edge_out.at[mine(s)],
             out_send.at[i],
             out_recv.at[i],
-            peer(0, df, dr),
-        )
+            peer(0, i // 2, i % 2),
+        )
+        copy.start()
         outs.append(copy)
     out_local = pltpu.make_async_copy(out_mine.at[f], edge_out.at[mine(s)], local_sem.at[6])
     out_local.start()
@@ -267,60 +288,8 @@
         )
         copy.start()
         bils.append(copy)
-    for copy in outs:
-        copy.start()
-    grad_tri[pl.ds(s * bpd, bpd)] = bil_mine[f]
-    chain[0] = jnp.zeros((half_c, rows_b), F32)
-    for copy in bils:
-        copy.wait_recv()
-
-    def backward(n, _):
-        block = grad_tri[n]
-        parts = [mm(block, coef[n, k], 1, 0) for k in range(tiles)]
-        for k in range(tiles):
-            t = n * tiles + k
-            chain[t + 1] = parts[k] + chain[links[t]]
-        return 0
-
-    lax.fori_loop(0, blocks, backward, 0)
-    entries = blocks * tiles
-    for i in range(2 * n_edge):
-        for b in range(bpd):
-            block_id = (i // 2) * blocks + (2 * (i % 2) + orr) * bpd + b
-            pair_out[i, b] = chain[links[entries + block_id]]
-    pair = remote(pair_out, pair_in, pair_send, pair_recv, peer(0, 0, 1))
-    pair.start()
-    pair.wait_recv()
-    for i in range(2 * n_edge):
-        for b in range(bpd):
-            block_id = (i // 2) * blocks + (2 * (i % 2) + r) * bpd + b
-            red_out[i, b] = (chain[links[entries + block_id]] + pair_in[i, b]).astype(BF16)
-    reds = []
-    for i in range(1, 2 * n_edge):
-        d, df = i // 2, i % 2
-        slot = 2 * lax.rem(e + d, n_edge) + (of if df else f)
-        copy = remote(
-            red_out.at[slot], red_in.at[i], red_send.at[i], red_recv.at[i], peer(d, df, 0)
-        )
-        copy.start()
-        reds.append(copy)
-    for copy in reds:
-        copy.wait_recv()
-    near = red_out[2 * e + f].astype(F32)
-    far = red_in[1].astype(F32)
-    for d in range(1, n_edge):
-        near += red_in[2 * d].astype(F32)
-        far += red_in[2 * d + 1].astype(F32)
-    low = jnp.where(f == 0, near, far)
-    high = jnp.where(f == 0, far, near)
-    grad_down = jnp.concatenate(
-        [jnp.concatenate([low[b], high[b]], axis=0) for b in range(bpd)], axis=1
-    )
-    grad_pre = (grad_down * slope(pre_down)).astype(BF16)
-    grad_edge = (grad_hb.astype(F32) + mm(grad_pre, wd, 0, 1)).astype(BF16)
     for h in range(2):
-        ge[h] = grad_edge[:, h * cols : (h + 1) * cols]
-
+        ge[h] = grad_hb[:, h * cols : (h + 1) * cols]
     sends = []
     for j in range(spd):
         q = s * spd + j
@@ -354,6 +323,41 @@
                         copy.start()
 
                     sends.append((copy, q != e))
+    grad_tri[pl.ds(s * bpd, bpd)] = bil_mine[f]
+    chain[0] = jnp.zeros((half_c, rows_b), F32)
+    for copy in bils:
+        copy.wait_recv()
+
+    def backward(n, _):
+        block = grad_tri[n]
+        parts = [mm(block, coef[n, k], 1, 0) for k in range(tiles)]
+        for k in range(tiles):
+            t = n * tiles + k
+            chain[t + 1] = parts[k] + chain[links[t]]
+        return 0
+
+    lax.fori_loop(0, blocks, backward, 0)
+    entries = blocks * tiles
+    for i in range(2 * n_edge):
+        for b in range(bpd):
+            block_id = (i // 2) * blocks + (2 * (i % 2) + orr) * bpd + b
+            pair_out[i, b] = chain[links[entries + block_id]]
+    pair = remote(pair_out, pair_in, pair_send, pair_recv, peer(0, 0, 1))
+    pair.start()
+    pair.wait_recv()
+    for i in range(2 * n_edge):
+        for b in range(bpd):
+            block_id = (i // 2) * blocks + (2 * (i % 2) + r) * bpd + b
+            red_out[i, b] = (chain[links[entries + block_id]] + pair_in[i, b]).astype(BF16)
+    reds = []
+    for i in range(1, 2 * n_edge):
+        d, df = i // 2, i % 2
+        slot = 2 * lax.rem(e + d, n_edge) + (of if df else f)
+        copy = remote(
+            red_out.at[slot], red_in.at[i], red_send.at[i], red_recv.at[i], peer(d, df, 0)
+        )
+        copy.start()
+        reds.append(copy)
     fins = []
     for d in range(n_edge):
         p = lax.rem(e + n_edge - d, n_edge)
@@ -374,24 +378,86 @@
         )
         copy.start()
         fins.append(copy)
+    relay_rows = mine(2 * of + r)
+    outs[1].wait_recv()
+    relay = remote(
+        edge_out.at[relay_rows], edge_out.at[relay_rows], out_send.at[3], out_recv.at[3], peer(0, 0, 1)
+    )
+    relay.start()
+    for copy in reds:
+        copy.wait_recv()
+    near = red_out[2 * e + f].astype(F32)
+    far = red_in[1].astype(F32)
+    for d in range(1, n_edge):
+        near += red_in[2 * d].astype(F32)
+        far += red_in[2 * d + 1].astype(F32)
+    low = jnp.where(f == 0, near, far)
+    high = jnp.where(f == 0, far, near)
+    grad_down = jnp.concatenate(
+        [jnp.concatenate([low[b], high[b]], axis=0) for b in range(bpd)], axis=1
+    )
+    grad_pre = (grad_down * slope(pre_down)).astype(BF16)
+    given = []
+    for j in range(spd):
+        gp_mine[j] = grad_pre[:, j * span : (j + 1) * span]
+        q = s * spd + j
+        d = lax.rem(q - e + n_edge, n_edge)
+        for df in range(2):
+            for dr in range(2):
+                copy = remote(
+                    gp_mine.at[j],
+                    gp_in.at[e],
+                    gp_send.at[j, 2 * df + dr],
+                    gp_recv.at[d],
+                    (g, q, of if df else f, orr if dr else r),
+                )
+                if df or dr:
+                    copy.start()
+                    given.append((copy, None))
+                else:
+
+                    @pl.when(q == e)
+                    def _(j=j):
+                        gp_in[e] = gp_mine[j]
+
+                    @pl.when(q != e)
+                    def _(copy=copy):
+                        copy.start()
+
+                    given.append((copy, q != e))
+    local[7].wait()
+    for d in range(n_edge):
+        p = lax.rem(e + n_edge - d, n_edge)
+        fins[d].wait_recv()
+        wish = wanted[p] - (p * turned.shape[0] + e * span)
+        slot = lax.broadcasted_iota(jnp.int32, (span, span), 0)
+        pick = jnp.where(slot == wish, 1.0, 0.0).astype(BF16)
+        picks[d] = pick
+        hb_perm[d] = mm(pick, turned[pl.ds(p * span, span)], 0, 0).astype(BF16)
     writes = []
     for d in range(n_edge):
         p = lax.rem(e + n_edge - d, n_edge)
-        fins[d].wait_recv()
-        wish = wanted[p]
-        slot = lax.broadcasted_iota(jnp.int32, (span, span), 0)
-        pick = jnp.where(slot == wish, 1.0, 0.0).astype(BF16)
+        arrive = remote(gp_mine.at[0], gp_in.at[p], gp_send.at[0, 0], gp_recv.at[d], peer(0, 0, 1))
+        if d:
+            arrive.wait_recv()
+        else:
+
+            @pl.when(s != e // spd)
+            def _(arrive=arrive):
+                arrive.wait_recv()
+
+        moved = mm(gp_in[p], picks[d], 1, 0).astype(BF16)
         place = pl.ds(p * span, span)
-        grad_v[place] = mm(pick, turned[place], 0, 0).astype(BF16)
-        copy = pltpu.make_async_copy(grad_v.at[place], grad_out.at[place], local_sem.at[7 + d])
+        grad_v[place] = (hb_perm[d].astype(F32) + mm(moved, wd, 0, 0)).astype(BF16)
+        copy = pltpu.make_async_copy(grad_v.at[place], grad_out.at[place], local_sem.at[10 + d])
         copy.start()
         writes.append(copy)
-    for copy in outs:
-        copy.wait()
+    relay.wait_recv()
+    outs[0].wait_recv()
     out_local.wait()
-    for copy in xs + tabs + cores + tris + bils + [pair] + reds + fins:
+    for copy in xs + tabs + cores + tris + outs + [relay] + bils + [pair] + reds + fins:
         copy.wait_send()
-    for copy, when in sends:
+    for copy, when in sends + given:
         if when is None:
             copy.wait_send()
         else:
@@ -429,8 +495,7 @@
     order = jnp.arange(entries, dtype=jnp.int32)
     same = (asked[:, None] == mine[None, :]) & (order[None, :] < before[:, None])
     links = jnp.max(jnp.where(same, order[None, :] + 1, 0), axis=1)
-    wanted = (target_rows % span).reshape(n_edge, 1, span)
-    vmem = pl.BlockSpec(memory_space=pltpu.VMEM)
+    wanted = target_rows.reshape(n_edge, 1, span)
     smem = pl.BlockSpec(memory_space=pltpu.SMEM)
     hbm = pl.BlockSpec(memory_space=pl.ANY)
     dma = pltpu.SemaphoreType.DMA
@@ -439,12 +504,17 @@
     return pl.pallas_call(
         functools.partial(block_kernel, n_edge),
         out_shape=[jax.ShapeDtypeStruct((edges, cols), BF16)] * 2,
-        in_specs=[smem, smem, vmem, vmem] + [hbm] * 6,
+        in_specs=[smem, smem] + [hbm] * 8,
         out_specs=[hbm, hbm],
         scratch_shapes=[
             pltpu.VMEM((2, rows, cols), BF16),
+            pltpu.VMEM((rows, cols), BF16),
+            pltpu.VMEM((width, rows), F32),
+            pltpu.VMEM((width, rows), F32),
             pltpu.VMEM((2, rows, cols), BF16),
-            pltpu.VMEM((2,) + w_down.shape, BF16),
+            pltpu.VMEM(wanted.shape, jnp.int32),
+            pltpu.VMEM(w_bilinear.shape, BF16),
+            pltpu.VMEM(w_down.shape[::-1], BF16),
             pltpu.VMEM((2,) + w_up.shape, BF16),
             pltpu.VMEM(w_residual.shape, BF16),
             pltpu.VMEM(tile_coef.shape, BF16),
@@ -462,8 +532,12 @@
             pltpu.VMEM((2, rows, cols), BF16),
             pltpu.VMEM((2, rows, cols), BF16),
             pltpu.VMEM((edges, cols), BF16),
+            pltpu.VMEM((n_edge, span, span), BF16),
+            pltpu.VMEM((n_edge, span, cols), BF16),
+            pltpu.VMEM((rows // span, width, span), BF16),
+            pltpu.VMEM((n_edge, width, span), BF16),
             pltpu.VMEM((edges, cols), BF16),
-            dma((7 + n_edge,)),
+            dma((10 + n_edge,)),
             dma((4,)),
             dma((4,)),
             dma((n2,)),
@@ -485,18 +559,20 @@
             dma((n_edge,)),
             dma((n_edge,)),
             dma(()),
+            dma((rows // span, 4)),
+            dma((n_edge,)),
         ],
         compiler_params=pltpu.CompilerParams(
-            collective_id=0, has_side_effects=True, vmem_limit_bytes=40 * 1024 * 1024
+            collective_id=0, has_side_effects=True, vmem_limit_bytes=62 * 1024 * 1024
         ),
         name="interaction",
     )(
-        tile_source,
+        tile_source.T,
         links,
         wanted,
         w_bilinear,
         edge_embed,
-        w_down,
+        w_down.T,
         w_up,
         w_residual,
         tile_coef,
@@ -640,7 +716,7 @@
         P(("grp", "edge")),
         P(("grp", "edge"), "feat"),
     )
-    fits = mesh.shape["feat"] == 2 and mesh.shape["rep"] == 2
+    fits = mesh.shape["feat"] == 2 and mesh.shape["rep"] == 2 and mesh.shape["edge"] in (4, 8)
     return jax.shard_map(
         fused if fits else on_device,
         mesh=mesh,

time: 65.8 us -> 55 us (0.84); the launches traced: 64.6 us -> 54.7 us
  local copies, waits for them, and re-layouts: 10.5 us -> 4.66 us
  Pallas kernels: 51.8 us -> 48 us
    unnamed x16 -> x2, local copies, waits for them, and re-layouts: 9.6 us -> 3.74 us
    pallas_call x1, Pallas kernels: 51.8 us -> 48 us  [fused(): pl.pallas_call(functools.partial(block_kernel, n_edge), out_shape=[jax.Sh...]
    select_n x1 -> x0, other arithmetic: 0.7 us -> none  [fused(): wanted = (target_rows % span).reshape(n_edge, 1, span)]
where the time goes in v2:
time: 55 us; the launch traced here: 54.7 us
  Pallas kernels  48 us (87%)
  local copies, waits for them, and re-layouts  4.66 us (8%)
  other arithmetic  1.35 us (2%)
  between operations  0.66 us (1%)
    pallas_call x1, Pallas kernels, fused(): pl.pallas_call(functools.partial(block_kernel, n_edge), out_shape=[jax.Sh...  48 us
    unnamed x2, local copies, waits for them, and re-layouts  3.74 us
    reduce_max x1, other arithmetic, fused(): links = jnp.max(jnp.where(same, order[None, :] + 1, 0), axis=1)  1.27 us

profile of v2, /device:TPU:0, one launch (start us, length us, event | category | flops | bytes accessed | tf_op | source)
XLA Modules:
  0.0 54.7 jit_solution(15566703132716483751)
XLA Ops:
  0.7 0.8 %dynamic_slice.3 = s32[8,8]{0,1:T(8,128)S(1)} dynamic-slice(s32[32,16]{0,1:T(8,128)} %param.15, s32[]{:T(128)S(6)} %select_n.10, s32[]{:T(128)S(6)} %select_n.11), dynamic_slice_sizes={8,8} | dynamic-slice | bytes 516 | tf_op jit(solution)/shard_map/dynamic_slice | solution.py:486
  1.4 0.1 copy.12
  1.5 0.1 reshape.18
  1.6 0.1 pad_add_fusion
  1.7 1.3 %select_reduce_fusion.links = s32[96]{0:T(128)} fusion(s32[64]{0:T(128)S(1)} %iota_add_fusion, s32[96]{0:T(128)} %constant.21.clone.1, s32[96]{0:T(128)S(1)} %pad_add_fusion, s32[64]{0:T(128)S(1)} %reshape.18), kind=kLoop, calls=%fused_computation | loop fusion | flops 30624 | bytes 1664 | tf_op jit(solution)/shard_map/reduce_max | solution.py:497
  2.9 48.0 %interaction.1 = (bf16[1024,256]{1,0:T(8,128)(2,1)}, bf16[1024,256]{1,0:T(8,128)(2,1)}) custom-call(s32[16,32]{1,0:T(8,128)} %bitcast.4, s32[96]{0:T(128)} %select_reduce_fusion.links, s32[4,1,256]{2,1,0:T(1,128)} %bitcast.5, bf16[64,64]{1,0:T(8,128)(2,1)} %bil_hbm.1, bf16[1024,256]{1,0:T(8,128)(2,1)} %edge_hbm.1, bf16[64,256]{1,0:T(8,128)(2,1)} %bitcast.3, ...), custom_call_target="tpu_custom_call" | custom-call | tf_op jit(solution)/shard_map/interaction/pallas_call | solution.py:504
  50.9 1.9 %copy.15 = bf16[1024,256]{1,0:T(8,128)(2,1)} copy(bf16[1024,256]{1,0:T(8,128)(2,1)} %get-tuple-element.4) | data formatting | bytes 1048576
  52.8 1.9 %copy.16 = bf16[1024,256]{1,0:T(8,128)(2,1)} copy(bf16[1024,256]{1,0:T(8,128)(2,1)} %get-tuple-element.5) | data formatting | bytes 1048576
  (2 shorter events, 0.0 us)

commit v3 on v2

--- a/solution.py
+++ b/solution.py
@@ -23,8 +23,7 @@
 
 def block_kernel(
     n_edge,
-    source,
-    links,
+    source_hbm,
     wanted_hbm,
     bil_hbm,
     edge_hbm,
@@ -62,6 +61,11 @@
     turned,
     picks,
     hb_perm,
+    source,
+    seen,
+    newest,
+    before,
+    last,
     gp_mine,
     gp_in,
     grad_v,
@@ -127,6 +131,7 @@
         pltpu.make_async_copy(bil_hbm, w_bil, local_sem.at[7]),
         pltpu.make_async_copy(wanted_hbm, wanted, local_sem.at[8]),
         pltpu.make_async_copy(edge_hbm.at[partner_rows], emb_x, local_sem.at[9]),
+        pltpu.make_async_copy(source_hbm, source, local_sem.at[10]),
     ]
     for copy in local:
         copy.start()
@@ -186,6 +191,23 @@
     xs[1].start()
     xs[2].start()
     table[region(e, s)] = down_mine[f]
+    local[9].wait()
+    entries = blocks * tiles
+    lanes = newest.shape[1]
+    ids = lax.broadcasted_iota(jnp.int32, (1, lanes), 1)
+    latest = jnp.zeros((1, lanes), jnp.int32)
+    for t in range(entries):
+        hit = ids == source[r * tiles + t % tiles, e * blocks + t // tiles]
+        seen[t : t + 1, :] = jnp.where(hit, latest, 0)
+        latest = jnp.where(hit, t + 1, latest)
+    newest[...] = latest
+    seen[...] = jnp.broadcast_to(jnp.max(seen[...], axis=1, keepdims=True), seen.shape)
+    lists = [
+        pltpu.make_async_copy(seen, before, local_sem.at[11]),
+        pltpu.make_async_copy(newest, last, local_sem.at[12]),
+    ]
+    for copy in lists:
+        copy.start()
     cores = [own]
     for i in range(1, 2 * n_edge):
         d, df = i // 2, i % 2
@@ -325,6 +347,8 @@
                     sends.append((copy, q != e))
     grad_tri[pl.ds(s * bpd, bpd)] = bil_mine[f]
     chain[0] = jnp.zeros((half_c, rows_b), F32)
+    for copy in lists:
+        copy.wait()
     for copy in bils:
         copy.wait_recv()
 
@@ -333,22 +357,21 @@
         parts = [mm(block, coef[n, k], 1, 0) for k in range(tiles)]
         for k in range(tiles):
             t = n * tiles + k
-            chain[t + 1] = parts[k] + chain[links[t]]
+            chain[t + 1] = parts[k] + chain[before[t, 0]]
         return 0
 
     lax.fori_loop(0, blocks, backward, 0)
-    entries = blocks * tiles
     for i in range(2 * n_edge):
         for b in range(bpd):
             block_id = (i // 2) * blocks + (2 * (i % 2) + orr) * bpd + b
-            pair_out[i, b] = chain[links[entries + block_id]]
+            pair_out[i, b] = chain[last[0, block_id]]
     pair = remote(pair_out, pair_in, pair_send, pair_recv, peer(0, 0, 1))
     pair.start()
     pair.wait_recv()
     for i in range(2 * n_edge):
         for b in range(bpd):
             block_id = (i // 2) * blocks + (2 * (i % 2) + r) * bpd + b
-            red_out[i, b] = (chain[links[entries + block_id]] + pair_in[i, b]).astype(BF16)
+            red_out[i, b] = (chain[last[0, block_id]] + pair_in[i, b]).astype(BF16)
     reds = []
     for i in range(1, 2 * n_edge):
         d, df = i // 2, i % 2
@@ -449,7 +472,7 @@
         moved = mm(gp_in[p], picks[d], 1, 0).astype(BF16)
         place = pl.ds(p * span, span)
         grad_v[place] = (hb_perm[d].astype(F32) + mm(moved, wd, 0, 0)).astype(BF16)
-        copy = pltpu.make_async_copy(grad_v.at[place], grad_out.at[place], local_sem.at[10 + d])
+        copy = pltpu.make_async_copy(grad_v.at[place], grad_out.at[place], local_sem.at[13 + d])
         copy.start()
         writes.append(copy)
     relay.wait_recv()
@@ -483,28 +506,17 @@
     span = edges // n_edge
     n_blocks = n_edge * blocks
     entries = blocks * tiles
-    mine = lax.dynamic_slice(
-        tile_source,
-        (lax.axis_index("edge") * blocks, lax.axis_index("rep") * tiles),
-        (blocks, tiles),
-    ).reshape(entries)
-    asked = jnp.concatenate([mine, jnp.arange(n_blocks, dtype=jnp.int32)])
-    before = jnp.concatenate(
-        [jnp.arange(entries, dtype=jnp.int32), jnp.full((n_blocks,), entries, jnp.int32)]
-    )
-    order = jnp.arange(entries, dtype=jnp.int32)
-    same = (asked[:, None] == mine[None, :]) & (order[None, :] < before[:, None])
-    links = jnp.max(jnp.where(same, order[None, :] + 1, 0), axis=1)
+    lanes = -(-n_blocks // 128) * 128
     wanted = target_rows.reshape(n_edge, 1, span)
-    smem = pl.BlockSpec(memory_space=pltpu.SMEM)
+    fixed = pl.BlockSpec(memory_space=pltpu.HBM)
     hbm = pl.BlockSpec(memory_space=pl.ANY)
     dma = pltpu.SemaphoreType.DMA
     tile = (bpd, half_c, rows_b)
     n2 = 2 * n_edge
     return pl.pallas_call(
         functools.partial(block_kernel, n_edge),
-        out_shape=[jax.ShapeDtypeStruct((edges, cols), BF16)] * 2,
-        in_specs=[smem, smem] + [hbm] * 8,
+        out_shape=[pltpu.VMEM((edges, cols), BF16)] * 2,
+        in_specs=[fixed] * 9,
         out_specs=[hbm, hbm],
         scratch_shapes=[
             pltpu.VMEM((2, rows, cols), BF16),
@@ -534,10 +546,15 @@
             pltpu.VMEM((edges, cols), BF16),
             pltpu.VMEM((n_edge, span, span), BF16),
             pltpu.VMEM((n_edge, span, cols), BF16),
+            pltpu.SMEM(tile_source.shape[::-1], jnp.int32),
+            pltpu.VMEM((entries, lanes), jnp.int32),
+            pltpu.VMEM((1, lanes), jnp.int32),
+            pltpu.SMEM((entries, lanes), jnp.int32),
+            pltpu.SMEM((1, lanes), jnp.int32),
             pltpu.VMEM((rows // span, width, span), BF16),
             pltpu.VMEM((n_edge, width, span), BF16),
             pltpu.VMEM((edges, cols), BF16),
-            dma((10 + n_edge,)),
+            dma((13 + n_edge,)),
             dma((4,)),
             dma((4,)),
             dma((n2,)),
@@ -563,12 +580,11 @@
             dma((n_edge,)),
         ],
         compiler_params=pltpu.CompilerParams(
-            collective_id=0, has_side_effects=True, vmem_limit_bytes=62 * 1024 * 1024
+            collective_id=0, has_side_effects=True, vmem_limit_bytes=60 * 1024 * 1024
         ),
         name="interaction",
     )(
         tile_source.T,
-        links,
         wanted,
         w_bilinear,
         edge_embed,

time: 55 us -> 49.1 us (0.89)
  local copies, waits for them, and re-layouts: 4.66 us -> 1.59 us
  other arithmetic: 1.35 us -> 0 us
  Pallas kernels: 48 us -> 46.8 us
    unnamed x2, local copies, waits for them, and re-layouts: 3.74 us -> 1.59 us
    reduce_max x1 -> x0, other arithmetic: 1.27 us -> none  [fused(): links = jnp.max(jnp.where(same, order[None, :] + 1, 0), axis=1)]
    pallas_call x1, Pallas kernels: 48 us -> 46.8 us  [fused(): pl.pallas_call(functools.partial(block_kernel, n_edge), out_shape=[pltpu....]
    dynamic_slice x2 -> x0, local copies, waits for them, and re-layouts: 0.84 us -> none  [fused(): lax.dynamic_slice(tile_source, (lax.axis_index('edge') * blocks, lax.axis...]
where the time goes in v3:
time: 49.1 us; the launch traced here: 49 us
  Pallas kernels  46.8 us (95%)
  local copies, waits for them, and re-layouts  1.59 us (3%)
  between operations  0.64 us (1%)
    pallas_call x1, Pallas kernels, fused(): pl.pallas_call(functools.partial(block_kernel, n_edge), out_shape=[pltpu....  46.8 us
    unnamed x2, local copies, waits for them, and re-layouts  1.59 us

profile of v3, /device:TPU:0, one launch (start us, length us, event | category | flops | bytes accessed | tf_op | source)
XLA Modules:
  0.0 49.0 jit_solution(14333438795539475045)
XLA Ops:
  0.6 46.8 %interaction.1 = (bf16[1024,256]{1,0:T(8,128)(2,1)S(1)}, bf16[1024,256]{1,0:T(8,128)(2,1)S(1)}) custom-call(s32[16,32]{1,0:T(8,128)} %bitcast.4, s32[4,1,256]{2,1,0:T(1,128)} %bitcast.5, bf16[64,64]{1,0:T(8,128)(2,1)} %bil_hbm.1, bf16[1024,256]{1,0:T(8,128)(2,1)} %edge_hbm.1, bf16[64,256]{1,0:T(8,128)(2,1)} %bitcast.3, bf16[64,256]{1,0:T(8,128)(2,1)} %up_hbm.1, ...), custom_call_target="tpu_custom_call" | custom-call | tf_op jit(solution)/shard_map/interaction/pallas_call | solution.py:516
  47.4 0.8 %copy.13 = bf16[1024,256]{1,0:T(8,128)(2,1)} copy(bf16[1024,256]{1,0:T(8,128)(2,1)S(1)} %get-tuple-element.2) | data formatting | bytes 1048576
  48.2 0.8 %copy.14 = bf16[1024,256]{1,0:T(8,128)(2,1)} copy(bf16[1024,256]{1,0:T(8,128)(2,1)S(1)} %get-tuple-element.3) | data formatting | bytes 1048576

commit v4 on v3

--- a/solution.py
+++ b/solution.py
@@ -48,6 +48,7 @@
     down_mine,
     table,
     tri_part,
+    tri_out,
     tri_in,
     bil_mine,
     grad_tri,
@@ -68,7 +69,6 @@
     last,
     gp_mine,
     gp_in,
-    grad_v,
     local_sem,
     x_send,
     x_recv,
@@ -229,6 +229,7 @@
         for k in range(tiles):
             total += mm(table[source[r * tiles + k, e * blocks + n]], coef[n, k], 1, 1)
         tri_part[n] = total
+        tri_out[n] = total.astype(BF16)
         return 0
 
     lax.fori_loop(0, blocks, forward, 0)
@@ -237,7 +238,7 @@
         df, dr = i // 2, i % 2
         to = 2 * (of if df else f) + (orr if dr else r)
         copy = remote(
-            tri_part.at[pl.ds(to * bpd, bpd)],
+            tri_out.at[pl.ds(to * bpd, bpd)],
             tri_in.at[i],
             tri_send.at[i],
             tri_recv.at[i],
@@ -247,8 +248,8 @@
         tris.append(copy)
     for copy in tris:
         copy.wait_recv()
-    near = tri_part[pl.ds(s * bpd, bpd)] + tri_in[1]
-    far = tri_in[2] + tri_in[3]
+    near = tri_part[pl.ds(s * bpd, bpd)] + tri_in[1].astype(F32)
+    far = tri_in[2].astype(F32) + tri_in[3].astype(F32)
     low = jnp.where(f == 0, near, far)
     high = jnp.where(f == 0, far, near)
     tri = jnp.concatenate(
@@ -364,14 +365,14 @@
     for i in range(2 * n_edge):
         for b in range(bpd):
             block_id = (i // 2) * blocks + (2 * (i % 2) + orr) * bpd + b
-            pair_out[i, b] = chain[last[0, block_id]]
+            pair_out[i, b] = chain[last[0, block_id]].astype(BF16)
     pair = remote(pair_out, pair_in, pair_send, pair_recv, peer(0, 0, 1))
     pair.start()
     pair.wait_recv()
     for i in range(2 * n_edge):
         for b in range(bpd):
             block_id = (i // 2) * blocks + (2 * (i % 2) + r) * bpd + b
-            red_out[i, b] = (chain[last[0, block_id]] + pair_in[i, b]).astype(BF16)
+            red_out[i, b] = (chain[last[0, block_id]] + pair_in[i, b].astype(F32)).astype(BF16)
     reds = []
     for i in range(1, 2 * n_edge):
         d, df = i // 2, i % 2
@@ -381,32 +382,6 @@
         )
         copy.start()
         reds.append(copy)
-    fins = []
-    for d in range(n_edge):
-        p = lax.rem(e + n_edge - d, n_edge)
-        place = pl.ds(p * span + r * hs, hs)
-        arrive = remote(
-            turned.at[place], turned.at[place], ge_send.at[0, 0], ge_recv.at[d], peer(0, 0, 1)
-        )
-        if d:
-            arrive.wait_recv()
-        else:
-
-            @pl.when(s != e // spd)
-            def _(arrive=arrive):
-                arrive.wait_recv()
-
-        copy = remote(
-            turned.at[place], turned.at[place], fin_send.at[d], fin_recv.at[d], peer(0, 0, 1)
-        )
-        copy.start()
-        fins.append(copy)
-    relay_rows = mine(2 * of + r)
-    outs[1].wait_recv()
-    relay = remote(
-        edge_out.at[relay_rows], edge_out.at[relay_rows], out_send.at[3], out_recv.at[3], peer(0, 0, 1)
-    )
-    relay.start()
     for copy in reds:
         copy.wait_recv()
     near = red_out[2 * e + f].astype(F32)
@@ -448,6 +423,32 @@
                         copy.start()
 
                     given.append((copy, q != e))
+    fins = []
+    for d in range(n_edge):
+        p = lax.rem(e + n_edge - d, n_edge)
+        place = pl.ds(p * span + r * hs, hs)
+        arrive = remote(
+            turned.at[place], turned.at[place], ge_send.at[0, 0], ge_recv.at[d], peer(0, 0, 1)
+        )
+        if d:
+            arrive.wait_recv()
+        else:
+
+            @pl.when(s != e // spd)
+            def _(arrive=arrive):
+                arrive.wait_recv()
+
+        copy = remote(
+            turned.at[place], turned.at[place], fin_send.at[d], fin_recv.at[d], peer(0, 0, 1)
+        )
+        copy.start()
+        fins.append(copy)
+    relay_rows = mine(2 * of + r)
+    outs[1].wait_recv()
+    relay = remote(
+        edge_out.at[relay_rows], edge_out.at[relay_rows], out_send.at[3], out_recv.at[3], peer(0, 0, 1)
+    )
+    relay.start()
     local[7].wait()
     for d in range(n_edge):
         p = lax.rem(e + n_edge - d, n_edge)
@@ -457,7 +458,6 @@
         pick = jnp.where(slot == wish, 1.0, 0.0).astype(BF16)
         picks[d] = pick
         hb_perm[d] = mm(pick, turned[pl.ds(p * span, span)], 0, 0).astype(BF16)
-    writes = []
     for d in range(n_edge):
         p = lax.rem(e + n_edge - d, n_edge)
         arrive = remote(gp_mine.at[0], gp_in.at[p], gp_send.at[0, 0], gp_recv.at[d], peer(0, 0, 1))
@@ -471,10 +471,7 @@
 
         moved = mm(gp_in[p], picks[d], 1, 0).astype(BF16)
         place = pl.ds(p * span, span)
-        grad_v[place] = (hb_perm[d].astype(F32) + mm(moved, wd, 0, 0)).astype(BF16)
-        copy = pltpu.make_async_copy(grad_v.at[place], grad_out.at[place], local_sem.at[13 + d])
-        copy.start()
-        writes.append(copy)
+        grad_out[place] = (hb_perm[d].astype(F32) + mm(moved, wd, 0, 0)).astype(BF16)
     relay.wait_recv()
     outs[0].wait_recv()
     out_local.wait()
@@ -488,9 +485,6 @@
             @pl.when(when)
             def _(copy=copy):
                 copy.wait_send()
-
-    for copy in writes:
-        copy.wait()
 
 
 def fused(
@@ -517,7 +511,7 @@
         functools.partial(block_kernel, n_edge),
         out_shape=[pltpu.VMEM((edges, cols), BF16)] * 2,
         in_specs=[fixed] * 9,
-        out_specs=[hbm, hbm],
+        out_specs=[hbm, pl.BlockSpec(memory_space=pltpu.VMEM)],
         scratch_shapes=[
             pltpu.VMEM((2, rows, cols), BF16),
             pltpu.VMEM((rows, cols), BF16),
@@ -533,12 +527,13 @@
             pltpu.VMEM((2,) + tile, BF16),
             pltpu.VMEM((n_blocks, half_c, rows_b), BF16),
             pltpu.VMEM((blocks, half_c, rows_b), F32),
-            pltpu.VMEM((4,) + tile, F32),
+            pltpu.VMEM((blocks, half_c, rows_b), BF16),
+            pltpu.VMEM((4,) + tile, BF16),
             pltpu.VMEM((2,) + tile, BF16),
             pltpu.VMEM((blocks, half_c, rows_b), BF16),
             pltpu.VMEM((entries + 1, half_c, rows_b), F32),
-            pltpu.VMEM((n2,) + tile, F32),
-            pltpu.VMEM((n2,) + tile, F32),
+            pltpu.VMEM((n2,) + tile, BF16),
+            pltpu.VMEM((n2,) + tile, BF16),
             pltpu.VMEM((n2,) + tile, BF16),
             pltpu.VMEM((n2,) + tile, BF16),
             pltpu.VMEM((2, rows, cols), BF16),
@@ -553,8 +548,7 @@
             pltpu.SMEM((1, lanes), jnp.int32),
             pltpu.VMEM((rows // span, width, span), BF16),
             pltpu.VMEM((n_edge, width, span), BF16),
-            pltpu.VMEM((edges, cols), BF16),
-            dma((13 + n_edge,)),
+            dma((13,)),
             dma((4,)),
             dma((4,)),
             dma((n2,)),

time: 49.1 us -> 48.2 us (0.982)
  Pallas kernels: 46.8 us -> 45.8 us
    pallas_call x1, Pallas kernels: 46.8 us -> 45.8 us  [fused(): pl.pallas_call(functools.partial(block_kernel, n_edge), out_shape=[pltpu....]
where the time goes in v4:
time: 48.2 us; the launch traced here: 48.1 us
  Pallas kernels  45.8 us (95%)
  local copies, waits for them, and re-layouts  1.59 us (3%)
  between operations  0.64 us (1%)
    pallas_call x1, Pallas kernels, fused(): pl.pallas_call(functools.partial(block_kernel, n_edge), out_shape=[pltpu....  45.8 us
    unnamed x2, local copies, waits for them, and re-layouts  1.59 us

profile of v4, /device:TPU:0, one launch (start us, length us, event | category | flops | bytes accessed | tf_op | source)
XLA Modules:
  0.0 48.1 jit_solution(2092302432039415044)
XLA Ops:
  0.6 45.8 %interaction.1 = (bf16[1024,256]{1,0:T(8,128)(2,1)S(1)}, bf16[1024,256]{1,0:T(8,128)(2,1)S(1)}) custom-call(s32[16,32]{1,0:T(8,128)} %bitcast.4, s32[4,1,256]{2,1,0:T(1,128)} %bitcast.5, bf16[64,64]{1,0:T(8,128)(2,1)} %bil_hbm.1, bf16[1024,256]{1,0:T(8,128)(2,1)} %edge_hbm.1, bf16[64,256]{1,0:T(8,128)(2,1)} %bitcast.3, bf16[64,256]{1,0:T(8,128)(2,1)} %up_hbm.1, ...), custom_call_target="tpu_custom_call" | custom-call | tf_op jit(solution)/shard_map/interaction/pallas_call | solution.py:510
  46.5 0.8 %copy.13 = bf16[1024,256]{1,0:T(8,128)(2,1)} copy(bf16[1024,256]{1,0:T(8,128)(2,1)S(1)} %get-tuple-element.2) | data formatting | bytes 1048576
  47.3 0.8 %copy.14 = bf16[1024,256]{1,0:T(8,128)(2,1)} copy(bf16[1024,256]{1,0:T(8,128)(2,1)S(1)} %get-tuple-element.3) | data formatting | bytes 1048576
